TPU v7x, 32 devices: a whole 2x2x4 slice. The times are simulated.
32 devices in a mesh: task: 4 (over y, x), dp: 4 (over z), tensor: 2 (over core).
Axes of the slice: x: 2, y: 2, z: 4, core: 2. Of those that a mesh axis runs over, the one named last changes fastest.
Arguments:
- queries: bfloat16 [4, 2400, 768], P('task', 'dp'), may hold values from -6 to 6
- memory: bfloat16 [4, 28800, 768], P('task', 'dp'), may hold values from -6 to 6
- cotangent: bfloat16 [4, 2400, 768], P('task', 'dp'), may hold values from -6 to 6
- matches: int32 [4, 24, 100], P('task', 'dp'), may hold values from 0 to 99, each once within a row
- counts: int32 [4, 24], P('task', 'dp'), may hold values from 1 to 100
- task_order: int32 [4], replicated, may hold values from 0 to 3, each once
- params: bfloat16 [768, 16, 768], P(None, None, 'tensor'), may hold values from -1.875 to 1.875
- head_bias: bfloat16 [8, 768], P(None, 'tensor'), may hold values from -3 to 3
- row_bias: bfloat16 [3, 2, 768], replicated, may hold values from -3 to 3
- norm_gain: bfloat16 [3, 768], replicated, may hold values from 0.5 to 1.5
Outputs:
- block_out: bfloat16 [4, 2400, 768], P('task', 'dp')
- query_grad: bfloat16 [4, 2400, 768], P('task', ('dp', 'tensor'))
- memory_grad: bfloat16 [4, 28800, 768], P('task', ('dp', 'tensor'))
- param_update: float32 [768, 16, 768], P('dp', None, 'tensor')
- head_bias_update: float32 [8, 768], P(None, 'tensor')
- row_bias_update: float32 [3, 2, 768], replicated
- gain_update: float32 [3, 768], replicated
- gram: float32 [4, 4], replicated
Inputs may be any that keep to these rules, and one draw needn't show every extreme that they name: `matches`: for each image, a permutation of the 100 query slots; only the first counts entries name matched queries. `task_order`: a permutation of the indices 0 to 3.
All inputs are finite; a program needn't handle non-finite values.
Results may differ from a plain program's by a relative error of at most 0.015.
Values may be sent and summed in bfloat16 or wider, within the bound.
A program may use at most 256 MiB of HBM per device.

v0:
```python
import functools

import jax
import jax.numpy as jnp
from jax import lax
from jax.experimental import pallas as pl
from jax.experimental.pallas import tpu as pltpu
from jax.sharding import PartitionSpec as P

HD = 64
GROUP = 4
SLAB = GROUP * HD
BF = jnp.bfloat16
F32 = jnp.float32
MESH_ID = pl.DeviceIdType.MESH
highest = lax.Precision.HIGHEST
VMEM_LIMIT = 63 * 2**20


def combine_weights(gram_matrix, order_list):
    task_count = gram_matrix.shape[0]
    task_index = jnp.arange(task_count, dtype=jnp.int32)
    summed = jnp.zeros((task_count,), F32)
    for own_task in range(task_count):
        coeffs = (task_index == own_task).astype(F32)
        for position in range(task_count):
            chosen = (task_index == order_list[position]).astype(F32)
            column = jnp.sum(gram_matrix * chosen[None, :], axis=1)
            inner_dot = jnp.sum(coeffs * column)
            square = jnp.sum(chosen * column)
            others = (order_list[position] != own_task).astype(F32)
            coeffs = coeffs - others * jnp.minimum(inner_dot, 0.0) / (square + 1e-06) * chosen
        summed = summed + coeffs
    return summed


def mm(a, b):
    return jnp.dot(a, b, preferred_element_type=F32)


def mm_nt(a, b):
    return lax.dot_general(a, b, (((1,), (1,)), ((), ())), preferred_element_type=F32)


def mm_tn(a, b):
    return lax.dot_general(a, b, (((0,), (0,)), ((), ())), preferred_element_type=F32)


def row_of(row_ref, which):
    return row_ref[which // 2, which % 2 : which % 2 + 1].astype(F32)


def gain_of(gain_ref, which):
    return gain_ref[which : which + 1].astype(F32)


def norm_parts(residual):
    row_mean = jnp.mean(residual, axis=-1, keepdims=True)
    centred = residual - row_mean
    variance = jnp.mean(centred * centred, axis=-1, keepdims=True)
    scale = lax.rsqrt(variance + 1e-05)
    return centred * scale, scale


def norm_back(normed, scale, gain_row, grad):
    scaled = grad * gain_row
    first = jnp.mean(scaled, axis=-1, keepdims=True)
    second = jnp.mean(scaled * normed, axis=-1, keepdims=True)
    return scale * (scaled - first - normed * second)


def rows_sum(value):
    return jnp.sum(value, axis=0, keepdims=True)


def gelu_tanh(hidden):
    square = hidden * hidden
    tanh = jnp.tanh(hidden * (0.7978845608028654 + 0.7978845608028654 * 0.044715 * square))
    half = 0.5 * (1.0 + tanh)
    inner = 0.7978845608028654 + 0.7978845608028654 * 3 * 0.044715 * square
    return hidden * half, half + 0.5 * hidden * (1.0 - tanh * tanh) * inner


def head_mask(head, rows, dtype):
    lane = lax.broadcasted_iota(jnp.int32, (rows, SLAB), 1)
    return (lane // HD == head).astype(F32).astype(dtype)


def stack_heads(slab):
    return jnp.concatenate(
        [slab * head_mask(head, slab.shape[0], slab.dtype) for head in range(GROUP)], axis=0
    )


def unstack_heads(stacked):
    rows = stacked.shape[0] // GROUP
    total = None
    for head in range(GROUP):
        part = stacked[head * rows : (head + 1) * rows] * head_mask(head, rows, stacked.dtype)
        total = part if total is None else total + part
    return total


def scores_of(query_stack, key_slab, valid):
    scores = mm_nt(key_slab, query_stack)
    if valid < key_slab.shape[0]:
        row = lax.broadcasted_iota(jnp.int32, scores.shape, 0)
        scores = jnp.where(row < valid, scores, -1e30)
    return scores


def attend(query_slab, key_slab, value_slab, valid):
    scores = scores_of(stack_heads(query_slab * HD ** (-0.5)), key_slab, valid)
    row_max = jnp.max(scores, axis=0, keepdims=True)
    exps = jnp.exp(scores - row_max)
    total = jnp.sum(exps, axis=0, keepdims=True)
    probs = (exps * (1.0 / total)).astype(BF)
    mixed = unstack_heads(mm_tn(value_slab, probs).T)
    return mixed, row_max + jnp.log(total)


def attend_back(query_slab, key_slab, value_slab, log_total, grad_slab, valid):
    query_stack = stack_heads(query_slab * HD ** (-0.5))
    grad_stack = stack_heads(grad_slab)
    probs = jnp.exp(scores_of(query_stack, key_slab, valid) - log_total)
    grad_value = mm(probs.astype(BF), grad_stack)
    grad_probs = mm_nt(value_slab, grad_stack)
    inner = jnp.sum(probs * grad_probs, axis=0, keepdims=True)
    grad_scores = (probs * (grad_probs - inner)).astype(BF)
    grad_key = mm(grad_scores, query_stack)
    grad_query = unstack_heads(mm_tn(key_slab, grad_scores).T) * HD ** (-0.5)
    return grad_query.astype(BF), grad_key.astype(BF), grad_value.astype(BF)


KEY_TILE = 400


def attend_back_tiles(
    query_slab, key_ref, value_ref, log_total, grad_slab, mixed_slab, key_grad_ref, value_grad_ref
):
    query_stack = stack_heads(query_slab * HD ** (-0.5))
    grad_stack = stack_heads(grad_slab)
    product = stack_heads(grad_slab.astype(F32) * mixed_slab.astype(F32))
    high = product.astype(BF)
    low = (product - high.astype(F32)).astype(BF)
    ones = jnp.ones((8, SLAB), BF)
    inner = (mm_nt(ones, high) + mm_nt(ones, low))[0:1]
    keys = key_ref.shape[0]
    size = KEY_TILE if keys % KEY_TILE == 0 else keys

    def tile(index, grad_query):
        rows = pl.ds(pl.multiple_of(index * size, size), size)
        key, value = key_ref[rows], value_ref[rows]
        probs = jnp.exp(mm_nt(key, query_stack) - log_total)
        grad_scores = (probs * (mm_nt(value, grad_stack) - inner)).astype(BF)
        value_grad_ref[rows] = mm(probs.astype(BF), grad_stack).astype(BF)
        key_grad_ref[rows] = mm(grad_scores, query_stack).astype(BF)
        return grad_query + mm_tn(key, grad_scores)

    grad_query = lax.fori_loop(
        0, keys // size, tile, jnp.zeros((SLAB, query_stack.shape[0]), F32)
    )
    return (unstack_heads(grad_query.T) * HD ** (-0.5)).astype(BF)


def pad_rows(source_ref, target_ref, images, valid):
    first = lax.axis_index("tensor") == 0
    padded = target_ref.shape[0] // images
    for image in range(images):
        here, there = (
            source_ref[(core * images + image) * valid : (core * images + image + 1) * valid]
            for core in range(2)
        )
        rows = jnp.where(first, here.astype(F32), there.astype(F32))
        fill = jnp.zeros((padded - valid, rows.shape[1]), F32)
        target_ref[image * padded : (image + 1) * padded] = jnp.concatenate(
            [rows, fill], axis=0
        ).astype(target_ref.dtype)


def send(source, target, send_sem, recv_sem, **device):
    return pltpu.make_async_remote_copy(
        source, target, send_sem, recv_sem, device_id=device, device_id_type=MESH_ID
    )


def start_kernel(
    images, valid, own_ref, bias_ref, queries_ref, cotangent_ref, row_ref, gain_ref,
    full_ref, head_ref, tokens_ref, own_cotangent_ref, qkv_ref, mixed_ref, total_ref, sum_ref,
    cross_query_ref, first, second, bias_own, bias_all, remote_send, remote_recv, local_sem, far_sem,
):
    step, steps = pl.program_id(0), pl.num_programs(0)
    other = 1 - lax.axis_index("tensor")
    rows, blocks, width = own_ref.shape
    parts = steps // 2
    near, far = pl.ds(0, width), pl.ds(width, width)
    lower, upper = pl.ds(0, blocks), pl.ds(blocks, blocks)

    def rows_of(part):
        return pl.ds(pl.multiple_of(part * rows, rows), rows)

    def first_copies(part):
        at = rows_of(part)
        return (
            send(
                first.at[:, at, near], first.at[:, at, far], remote_send.at[part],
                remote_recv.at[part], tensor=other,
            ),
            pltpu.make_async_copy(
                first.at[:, at, near], full_ref.at[lower, at, near], local_sem.at[part]
            ),
        )

    def second_copies(part):
        at = rows_of(part)
        return (
            send(
                second.at[:, at], full_ref.at[upper, at, far], remote_send.at[parts + part],
                remote_recv.at[parts + part], tensor=other,
            ),
            pltpu.make_async_copy(
                second.at[:, at], full_ref.at[upper, at, near], local_sem.at[parts + part]
            ),
        )

    bias_copy = send(
        bias_own, bias_all.at[:, far], remote_send.at[steps], remote_recv.at[steps], tensor=other
    )
    far_copy = pltpu.make_async_copy(first.at[:, :, far], full_ref.at[lower, :, far], far_sem)

    @pl.when(step == 0)
    def _():
        barrier = pltpu.get_barrier_semaphore()
        pl.semaphore_signal(barrier, inc=1, device_id={"tensor": other}, device_id_type=MESH_ID)
        pl.semaphore_wait(barrier, 1)
        bias_own[...] = jnp.zeros_like(bias_own)
        bias_own[0 : bias_ref.shape[0]] = bias_ref[...]
        bias_copy.start()
        bias_all[:, near] = bias_own[...]

    @pl.when(step < parts)
    def _():
        first[:, rows_of(step), near] = jnp.swapaxes(own_ref[...], 0, 1)
        for copy in first_copies(step):
            copy.start()

    @pl.when(step >= parts)
    def _():
        second[:, rows_of(step - parts)] = jnp.swapaxes(own_ref[...], 0, 1)
        for copy in second_copies(step - parts):
            copy.start()

    @pl.when(step == steps - 1)
    def _():
        pad_rows(queries_ref, tokens_ref, images, valid)
        pad_rows(cotangent_ref, own_cotangent_ref, images, valid)
        bias_copy.wait()
        head_ref[...] = bias_all[...]
        for part in range(parts):
            first_copies(part)[0].wait_recv()
        far_copy.start()
        self_forward(
            images, valid, tokens_ref, first, head_ref, row_ref, gain_ref, qkv_ref, mixed_ref,
            total_ref, sum_ref, cross_query_ref,
        )
        far_copy.wait()
        for part in range(parts):
            remote, local = first_copies(part)
            remote.wait_send()
            local.wait()
            for copy in second_copies(part):
                copy.wait()


def any_spec():
    return pl.BlockSpec(memory_space=pl.ANY)


def whole_spec():
    return pl.BlockSpec(memory_space=pltpu.VMEM)


def params_for(**keys):
    return pltpu.CompilerParams(vmem_limit_bytes=VMEM_LIMIT, **keys)


def place_of(index, groups, rows):
    image = index // groups
    group = index - image * groups
    if isinstance(index, int):
        return pl.ds(image * rows, rows), pl.ds(group * SLAB, SLAB)
    return (
        pl.ds(pl.multiple_of(image * rows, rows), rows),
        pl.ds(pl.multiple_of(group * SLAB, SLAB), SLAB),
    )


def self_forward(images, valid, tokens_ref, weight_ref, head_ref, row_ref, gain_ref, qkv_ref,
                 mixed_ref, total_ref, sum_ref, cross_query_ref):
    tokens = tokens_ref[...]
    rows = tokens.shape[0] // images
    width = tokens.shape[1]
    qkv_ref[0] = (mm(tokens, weight_ref[0]) + head_ref[0:1].astype(F32)).astype(BF)
    qkv_ref[1] = mm(tokens, weight_ref[1]).astype(BF)
    qkv_ref[2] = (mm(tokens, weight_ref[2]) + head_ref[1:2].astype(F32)).astype(BF)
    groups = width // SLAB

    for index in range(images * groups):
        at, lanes = place_of(index, groups, rows)
        mixed, log_total = attend(
            qkv_ref[0, at, lanes], qkv_ref[1, at, lanes], qkv_ref[2, at, lanes], valid
        )
        mixed_ref[at, lanes] = mixed.astype(BF)
        total_ref[index] = jnp.broadcast_to(log_total, total_ref.shape[1:])
    first_sum = tokens.astype(F32) + mm_nt(mixed_ref[...], weight_ref[3]) + row_of(row_ref, 0)
    sum_ref[...] = first_sum
    first_low = (norm_parts(first_sum)[0] * gain_of(gain_ref, 0) + row_of(row_ref, 1)).astype(BF)
    cross_query_ref[...] = (mm(first_low, weight_ref[4]) + head_ref[2:3].astype(F32)).astype(BF)


def cross_kernel(context_ref, query_ref, key_w_ref, value_w_ref, head_ref, key_ref, value_ref,
                 mixed_ref, total_ref):
    context = context_ref[...]
    for group in range(key_ref.shape[1] // SLAB):
        lanes = slice(group * SLAB, (group + 1) * SLAB)
        key_ref[:, lanes] = mm(context, key_w_ref[0, :, lanes]).astype(BF)
        value_ref[:, lanes] = (
            mm(context, value_w_ref[0, :, lanes]) + head_ref[3:4, lanes].astype(F32)
        ).astype(BF)
        mixed, log_total = attend(
            query_ref[:, lanes], key_ref[:, lanes], value_ref[:, lanes], key_ref.shape[0]
        )
        mixed_ref[:, lanes] = mixed.astype(BF)
        total_ref[group] = jnp.broadcast_to(log_total, total_ref.shape[1:])


def ffn_kernel(
    images, blocks, per, sum_ref, mixed_ref, cotangent_ref, matches_ref, counts_ref, cross_w_ref,
    weight_ref, head_ref, row_ref, gain_ref,
    block_ref, left_ref, right_ref, mixed_grad_ref, residual_ref, small_ref,
    second_sum, second_low, left, right, slope, branch, third_grad, hidden_bias, weights, left_sem,
    right_sem, weight_sem,
):
    step = pl.program_id(0)
    half_steps = blocks // per

    def weight_copies(first):
        at = pl.ds(first, per)
        return [
            pltpu.make_async_copy(
                weight_ref.at[pl.ds(8 + which * blocks + first, per)], weights.at[which, at],
                weight_sem.at[which, first // per],
            )
            for which in range(2)
        ]
    rows = sum_ref.shape[0] // images

    def left_copy(which):
        return pltpu.make_async_copy(left.at[which], left_ref.at[which], left_sem.at[which])

    def right_copy(which):
        return pltpu.make_async_copy(right.at[which], right_ref.at[which], right_sem.at[which])

    mixed_copy = pltpu.make_async_copy(
        mixed_ref, right_ref.at[2 * blocks], right_sem.at[2 * blocks]
    )

    @pl.when(step == 0)
    def _():
        for copy in weight_copies(0):
            copy.start()
        mixed_copy.start()
        first_out = norm_parts(sum_ref[...])[0] * gain_of(gain_ref, 0) + row_of(row_ref, 1)
        second = first_out + mm_nt(mixed_ref[...], cross_w_ref[0]) + row_of(row_ref, 2)
        second_sum[...] = second
        second_low[...] = (
            norm_parts(second)[0] * gain_of(gain_ref, 1) + row_of(row_ref, 3)
        ).astype(BF)
        branch[...] = jnp.zeros_like(branch)
        small_ref[...] = jnp.zeros_like(small_ref)
        hidden_bias[0:blocks] = head_ref[4 : 4 + blocks].astype(F32)
        left[0] = second_low[...].T
        left_copy(0).start()

    @pl.when(step < half_steps)
    def _():
        low = second_low[...]
        first = step * per
        copies = weight_copies(first)
        copies[0].wait()
        copies[1].wait()

        @pl.when(step + 1 < half_steps)
        def _():
            for copy in weight_copies(first + per):
                copy.start()

        pres = [
            mm(low, weights[0, first + k]) + hidden_bias[pl.ds(first + k, 1)] for k in range(per)
        ]
        total = branch[...]
        for k in range(per):
            act, grad = gelu_tanh(pres[k])
            act = act.astype(BF)
            slope[first + k] = grad
            right[blocks + first + k] = act
            right_copy(blocks + first + k).start()
            total = total + mm_nt(act, weights[1, first + k])
        branch[...] = total

    @pl.when(step == half_steps - 1)
    def _():
        second = norm_parts(second_sum[...])[0] * gain_of(gain_ref, 1) + row_of(row_ref, 3)
        third_sum = second + branch[...] + row_of(row_ref, 4)
        normed, scale = norm_parts(third_sum)
        block_ref[...] = (normed * gain_of(gain_ref, 2) + row_of(row_ref, 5)).astype(BF)
        count = matches_ref.shape[2]
        slot = lax.broadcasted_iota(jnp.int32, (rows, count), 0)
        box = lax.broadcasted_iota(jnp.int32, (rows, count), 1)
        grads = []
        for image in range(images):
            own = lax.axis_index("tensor") * images + image
            live = (matches_ref[0, pl.ds(own, 1)] == slot) & (box < counts_ref[0, own])
            mask = jnp.sum(jnp.where(live, 1.0, 0.0), axis=1, keepdims=True)
            cot = cotangent_ref[image * rows : (image + 1) * rows].astype(F32)
            grads.append(cot * mask)
        out_grad = jnp.concatenate(grads, axis=0)
        grad = norm_back(normed, scale, gain_of(gain_ref, 2), out_grad)
        third_grad[...] = grad
        left[1] = grad.astype(BF).T
        left_copy(1).start()
        small_ref[12:13] = rows_sum(grad)
        small_ref[13:14] = rows_sum(out_grad)
        small_ref[16:17] = rows_sum(out_grad * normed)
        branch[...] = jnp.zeros_like(branch)

    @pl.when(step >= half_steps)
    def _():
        ffn_low = third_grad[...].astype(BF)
        first = (step - half_steps) * per
        grads = [mm(ffn_low, weights[1, first + k]) for k in range(per)]
        total = branch[...]
        for k in range(per):
            grad_low = (grads[k] * slope[first + k]).astype(BF)
            right[first + k] = grad_low
            right_copy(first + k).start()
            small_ref[pl.ds(4 + first + k, 1)] = rows_sum(grad_low.astype(F32))
            total = total + mm_nt(grad_low, weights[0, first + k])
        branch[...] = total

    @pl.when(step == 2 * half_steps - 1)
    def _():
        second_in = third_grad[...] + branch[...]
        normed, scale = norm_parts(second_sum[...])
        grad = norm_back(normed, scale, gain_of(gain_ref, 1), second_in)
        residual_ref[...] = grad
        small_ref[10:11] = rows_sum(grad)
        small_ref[11:12] = rows_sum(second_in)
        small_ref[15:16] = rows_sum(second_in * normed)
        cross_low = grad.astype(BF)
        left[2] = cross_low.T
        left_copy(2).start()
        mixed_grad_ref[...] = mm(cross_low, cross_w_ref[0]).astype(BF)
        mixed_copy.wait()
        for which in range(3):
            left_copy(which).wait()
        for which in range(2 * blocks):
            right_copy(which).wait()


def cross_back_step(
    image, group, query_ref, key_ref, value_ref, total_ref, mixed_grad_ref, mixed_ref, small_ref,
    context_t, key_acc, value_acc, key_grad_ref, value_grad_ref, unit,
):
    grad_query = attend_back_tiles(
        query_ref[...], key_ref, value_ref, total_ref[0, 0:1], mixed_grad_ref[...], mixed_ref[...],
        key_grad_ref, value_grad_ref,
    )
    grad_key, grad_value = key_grad_ref[...], value_grad_ref[...]
    lanes = pl.ds(pl.multiple_of(group * SLAB, SLAB), SLAB)
    small_ref[2:3, lanes] += rows_sum(grad_query.astype(F32))
    small_ref[3:4, lanes] += rows_sum(grad_value.astype(F32))
    unit(0)
    key_wg = mm(context_t[...], grad_key)
    value_wg = mm(context_t[...], grad_value)

    @pl.when(image == 0)
    def _():
        key_acc[:, lanes] = key_wg
        value_acc[:, lanes] = value_wg

    @pl.when(image > 0)
    def _():
        key_acc[:, lanes] += key_wg
        value_acc[:, lanes] += value_wg

    unit(1)
    return grad_query


def cross_back_kernel(
    context_ref, query_ref, key_ref, value_ref, total_ref, mixed_grad_ref, mixed_ref, key_w_ref,
    value_w_ref, query_grad_ref, context_grad_ref, key_wg_ref, value_wg_ref, small_ref,
    context_t, acc, key_acc, value_acc, key_grad, value_grad,
):
    image, group = pl.program_id(0), pl.program_id(1)
    images, groups = pl.num_programs(0), pl.num_programs(1)

    @pl.when((image == 0) & (group == 0))
    def _():
        small_ref[...] = jnp.zeros_like(small_ref)

    @pl.when(group == 0)
    def _():
        context_t[...] = context_ref[...].T

    query_grad_ref[...] = cross_back_step(
        image, group, query_ref, key_ref, value_ref, total_ref, mixed_grad_ref, mixed_ref,
        small_ref, context_t, key_acc, value_acc, key_grad, value_grad, lambda part: None,
    )
    context_part = mm_nt(key_grad[...], key_w_ref[0]) + mm_nt(value_grad[...], value_w_ref[0])

    @pl.when(group == 0)
    def _():
        acc[...] = context_part

    @pl.when(group > 0)
    def _():
        acc[...] += context_part

    @pl.when(group == groups - 1)
    def _():
        context_grad_ref[...] = acc[...].astype(BF)

    @pl.when((image == images - 1) & (group == groups - 1))
    def _():
        key_wg_ref[...] = key_acc[...].astype(BF)
        value_wg_ref[...] = value_acc[...].astype(BF)


def self_back(
    images, valid, tokens_ref, weight_ref, row_ref, gain_ref, qkv_ref, mixed_ref, total_ref, sum_ref,
    residual_ref, cross_query_grad_ref, mixed_grad_ref, small_ref, qkv_grad, emit, unit, loop_unit,
    used,
):
    tokens = tokens_ref[...]
    rows = tokens.shape[0] // images
    width = tokens.shape[1]
    normed, scale = norm_parts(sum_ref[...])
    first_low = (normed * gain_of(gain_ref, 0) + row_of(row_ref, 1)).astype(BF)
    cross_query_grad = cross_query_grad_ref[...]
    first_low_t = first_low.T
    emit(4, lambda lanes: mm(first_low_t, cross_query_grad_ref[:, lanes]))
    unit()
    first_in = residual_ref[...] + mm_nt(cross_query_grad, weight_ref[4])
    first_grad = norm_back(normed, scale, gain_of(gain_ref, 0), first_in)
    small_ref[8:9] = rows_sum(first_grad)
    small_ref[9:10] = rows_sum(first_in)
    small_ref[14:15] = rows_sum(first_in * normed)
    self_low = first_grad.astype(BF)
    self_low_t = self_low.T
    emit(3, lambda lanes: mm(self_low_t, mixed_ref[:, lanes]))
    unit()
    mixed_grad_ref[...] = mm(self_low, weight_ref[3]).astype(BF)
    used()
    groups = width // SLAB

    def one(index, carry):
        at, lanes = place_of(index, groups, rows)
        grads = attend_back(
            qkv_ref[0, at, lanes], qkv_ref[1, at, lanes], qkv_ref[2, at, lanes],
            total_ref[index, 0:1], mixed_grad_ref[at, lanes], valid,
        )
        for which in range(3):
            qkv_grad[which, at, lanes] = grads[which]
        loop_unit(index)
        return carry

    lax.fori_loop(0, images * groups, one, 0)
    tokens_t = tokens.T
    total = first_grad
    for which in range(3):
        grad = qkv_grad[which]
        emit(which, lambda lanes, which=which: mm(tokens_t, qkv_grad[which, :, lanes]))
        if which != 1:
            unit()
        total = total + mm_nt(grad, weight_ref[which])
    small_ref[0:1] = rows_sum(qkv_grad[0].astype(F32))
    small_ref[1:2] = rows_sum(qkv_grad[2].astype(F32))
    return total


def self_back_kernel(
    images, valid, tokens_ref, weight_ref, row_ref, gain_ref, qkv_ref, mixed_ref, total_ref, sum_ref,
    residual_ref, cross_query_grad_ref, query_grad_ref, wg_ref, small_ref, qkv_grad, mixed_grad,
):
    small_ref[...] = jnp.zeros_like(small_ref)

    def emit(block, value):
        for lane in range(0, wg_ref.shape[2], SLAB):
            lanes = slice(lane, lane + SLAB)
            wg_ref[block, :, lanes] = value(lanes).astype(BF)

    query_grad_ref[...] = self_back(
        images, valid, tokens_ref, weight_ref, row_ref, gain_ref, qkv_ref, mixed_ref, total_ref,
        sum_ref, residual_ref, cross_query_grad_ref, mixed_grad, small_ref, qkv_grad, emit,
        lambda: None, lambda index: None, lambda: None,
    ).astype(BF)


def task_peers(tasks):
    me = lax.axis_index("task")
    return [lax.rem(me + shift, tasks) for shift in range(1, tasks)]


def task_senders(tasks):
    me = lax.axis_index("task")
    return [lax.rem(me + tasks - shift, tasks) for shift in range(1, tasks)]


def greet(depth, tasks):
    me = lax.axis_index("dp")
    barrier = pltpu.get_barrier_semaphore()
    other = 1 - lax.axis_index("tensor")
    for peer in task_peers(tasks):
        pl.semaphore_signal(barrier, inc=1, device_id={"task": peer}, device_id_type=MESH_ID)
        pl.semaphore_signal(
            barrier, inc=1, device_id={"task": peer, "tensor": other}, device_id_type=MESH_ID
        )
    for shift in range(1, depth):
        pl.semaphore_signal(
            barrier, inc=1, device_id={"dp": lax.rem(me + shift, depth)}, device_id_type=MESH_ID
        )
    pl.semaphore_signal(barrier, inc=1, device_id={"tensor": other}, device_id_type=MESH_ID)
    pl.semaphore_wait(barrier, 2 * (tasks - 1) + depth)


LAG = 2
SLOTS = 3
STAGES = 2


class Chain:
    def __init__(self, depth, tasks, refs):
        self.depth, self.tasks = depth, tasks
        (self.near, self.far, self.stage, self.passed, self.parts,
         self.far_send, self.far_recv, self.far_free, self.pass_send, self.pass_recv,
         self.part_send, self.part_recv) = refs
        self.chunks = self.passed.shape[1]
        self.rows, self.half = self.passed.shape[2:]
        self.me = lax.axis_index("dp")
        self.task = lax.axis_index("task")
        self.is_end = (self.me == 0) | (self.me == depth - 1)

    SCRATCH = 12

    @staticmethod
    def scratch(blocks, rows, half, tasks):
        chunks = 2 * blocks
        dma = pltpu.SemaphoreType.DMA
        return [
            pltpu.VMEM((2, chunks, rows, half), BF),
            pltpu.VMEM((SLOTS, 2, 2, rows, half), BF),
            pltpu.VMEM((STAGES, 2, 2, rows, half), BF),
            pltpu.VMEM((2, chunks, rows, half), BF),
            pltpu.VMEM((tasks, chunks, rows // tasks, half), BF),
            dma((STAGES,)),
            dma((SLOTS,)),
            pltpu.SemaphoreType.REGULAR,
            dma((2, chunks)),
            dma((2, chunks)),
            dma((blocks, tasks - 1)),
            dma((blocks, tasks - 1)),
        ]

    def far_copy(self, block):
        slot, stage = lax.rem(block, SLOTS), lax.rem(block, STAGES)
        return send(
            self.stage.at[stage], self.far.at[slot], self.far_send.at[stage], self.far_recv.at[slot],
            tensor=1 - lax.axis_index("tensor"),
        )

    def emit(self, block, value):
        block = jnp.int32(block)
        stage = lax.rem(block, STAGES)

        @pl.when(block >= STAGES)
        def _():
            self.far_copy(block).wait_send()

        @pl.when(block >= SLOTS)
        def _():
            pl.semaphore_wait(self.far_free, 1)

        def place(low, target):
            for way in range(2):
                for part in range(2):
                    row = (2 * way + part) * self.rows
                    target(way, part, low[row : row + self.rows])

        def slab(start):
            low = value(slice(start, start + SLAB)).astype(BF)
            own = max(min(self.half - start, SLAB), 0)
            if own:

                def keep(way, part, rows):
                    self.near[way, 2 * block + part, :, start : start + own] = rows

                place(low[:, :own], keep)
            if own < SLAB:
                first = start + own - self.half

                def give(way, part, rows):
                    self.stage[stage, way, part, :, first : first + SLAB - own] = rows

                place(low[:, own:], give)

        starts = range(0, 2 * self.half, SLAB)
        for start in starts:
            if start + SLAB > self.half:
                slab(start)
        self.far_copy(block).start()
        for start in starts:
            if start + SLAB <= self.half:
                slab(start)

    def absorb(self, block):
        block = jnp.int32(block)
        slot = lax.rem(block, SLOTS)
        self.far_copy(block).wait_recv()
        for way in range(2):
            chunks = pl.ds(2 * block, 2)
            self.near[way, chunks] = (
                self.near[way, chunks].astype(F32) + self.far[slot, way].astype(F32)
            ).astype(BF)

        @pl.when(block < self.chunks // 2 - SLOTS)
        def _():
            pl.semaphore_signal(
                self.far_free, inc=1, device_id={"tensor": 1 - lax.axis_index("tensor")},
                device_id_type=MESH_ID,
            )

    def pass_copy(self, way, chunk):
        piece = self.passed.at[way, chunk]
        target = self.me - 1 if way == 0 else self.me + 1
        return send(
            piece, piece, self.pass_send.at[way, chunk], self.pass_recv.at[way, chunk], dp=target
        )

    def part_rows(self, peer):
        size = self.rows // self.tasks
        return pl.ds(pl.multiple_of(peer * size, size), size)

    def part_copy(self, way, block, shift, peer):
        chunks = pl.ds(2 * block, 2)
        return send(
            self.passed.at[way, chunks, self.part_rows(peer)], self.parts.at[self.task, chunks],
            self.part_send.at[block, shift], self.part_recv.at[block, shift], task=peer,
        )

    def hops(self, way):
        return self.depth - 1 - self.me if way == 0 else self.me

    def units(self):
        return self.chunks + LAG * (self.depth - 1)

    def unit(self, index):
        for way in range(2):
            chunk = index - LAG * self.hops(way)

            @pl.when((chunk >= 0) & (chunk < self.chunks))
            def _(way=way, chunk=chunk):
                self.chunk_step(way, chunk)

    def chunk_step(self, way, chunk):
        first, last = self.hops(way) == 0, self.hops(way) == self.depth - 1
        block = chunk // 2
        own = self.near[way, chunk]

        @pl.when(first)
        def _():
            self.passed[way, chunk] = own

        @pl.when(jnp.logical_not(first))
        def _():
            self.pass_copy(way, chunk).wait_recv()
            self.passed[way, chunk] = (
                own.astype(F32) + self.passed[way, chunk].astype(F32)
            ).astype(BF)

        @pl.when(jnp.logical_not(last))
        def _():
            self.pass_copy(way, chunk).start()

        @pl.when(last & (chunk == 2 * block + 1))
        def _():
            for shift, peer in enumerate(task_peers(self.tasks)):
                self.part_copy(way, block, shift, peer).start()
            own_rows = self.part_rows(self.task)
            self.parts[self.task, chunk - 1] = self.passed[way, chunk - 1, own_rows]
            self.parts[self.task, chunk] = self.passed[way, chunk, own_rows]

    def wait_parts(self, block):
        for shift, peer in enumerate(task_senders(self.tasks)):
            landed = self.parts.at[peer, pl.ds(2 * block, 2)]
            send(
                landed, landed, self.part_send.at[block, shift], self.part_recv.at[block, shift],
                task=peer,
            ).wait_recv()

    def finish(self):
        def blocks(block, carry):
            for way in range(2):

                @pl.when(self.hops(way) != self.depth - 1)
                def _(way=way):
                    for part in range(2):
                        self.pass_copy(way, 2 * block + part).wait_send()

                @pl.when(self.hops(way) == self.depth - 1)
                def _(way=way):
                    for shift, peer in enumerate(task_peers(self.tasks)):
                        self.part_copy(way, block, shift, peer).wait_send()

            return carry

        lax.fori_loop(0, self.chunks // 2, blocks, 0)


def pairs_of(tasks):
    return [(a, b) for a in range(tasks) for b in range(a, tasks)]


def weights_of(gram, order_ref, tasks):
    totals = [0.0] * tasks
    for own in range(tasks):
        coeffs = [jnp.full_like(gram[0, 0], 1.0 if t == own else 0.0) for t in range(tasks)]
        for position in range(tasks):
            chosen = [
                jnp.where(order_ref[position] == t, 1.0, 0.0).astype(F32) for t in range(tasks)
            ]
            column = [sum(gram[t, j] * chosen[j] for j in range(tasks)) for t in range(tasks)]
            inner = sum(coeffs[t] * column[t] for t in range(tasks))
            square = sum(chosen[t] * column[t] for t in range(tasks))
            others = 1.0 - chosen[own]
            share = others * jnp.minimum(inner, 0.0) / (square + 1e-06)
            coeffs = [coeffs[t] - share * chosen[t] for t in range(tasks)]
        totals = [total + coeff for total, coeff in zip(totals, coeffs)]
    return totals


GROUPS = 4
UNITS = 2
TILE = 240


class ContextGrad:
    def __init__(self, key_grad, value_grad, weights, result, refs):
        self.grads, self.weights, self.result = (key_grad, value_grad), weights, result
        (self.staged, self.ring, self.done, self.staged_sem, self.ring_sem, self.done_sem) = refs
        self.tile = self.done.shape[1]
        self.tiles = result.shape[0] // self.tile

    SCRATCH = 6

    @staticmethod
    def scratch(keys, width):
        dma = pltpu.SemaphoreType.DMA
        return [
            pltpu.VMEM((2, keys, SLAB), BF),
            pltpu.VMEM((2, 2, width // SLAB, TILE, SLAB), BF),
            pltpu.VMEM((2, TILE, width), BF),
            dma((2,)),
            dma((2, 2)),
            dma((2,)),
        ]

    def staged_copies(self, image, group):
        keys = self.staged.shape[1]
        rows = pl.ds(pl.multiple_of(image * keys, keys), keys)
        return [
            pltpu.make_async_copy(
                self.staged.at[which], self.grads[which].at[group, rows], self.staged_sem.at[which]
            )
            for which in range(2)
        ]

    def put(self, image, group):
        for copy in self.staged_copies(image, group):
            copy.start()

    def settle(self):
        for copy in self.staged_copies(0, 0):
            copy.wait()

    def fetches(self, index):
        slot = lax.rem(index, 2)
        rows = pl.ds(pl.multiple_of(index * self.tile, self.tile), self.tile)
        return [
            pltpu.make_async_copy(
                self.grads[which].at[:, rows], self.ring.at[slot, which],
                self.ring_sem.at[slot, which],
            )
            for which in range(2)
        ]

    def store(self, index):
        slot = lax.rem(index, 2)
        rows = pl.ds(pl.multiple_of(index * self.tile, self.tile), self.tile)
        return pltpu.make_async_copy(
            self.done.at[slot], self.result.at[rows], self.done_sem.at[slot]
        )

    def compute(self, index):
        @pl.when(index < self.tiles)
        def _():
            for copy in self.fetches(index):
                copy.wait()

            @pl.when(index + 1 < self.tiles)
            def _():
                for copy in self.fetches(index + 1):
                    copy.start()

            @pl.when(index >= 2)
            def _():
                self.store(index - 2).wait()

            slot = lax.rem(index, 2)
            parts = [
                jnp.concatenate(
                    [self.ring[slot, which, group] for group in range(self.ring.shape[2])], axis=1
                )
                for which in range(2)
            ]
            total = mm_nt(parts[0], self.weights[0]) + mm_nt(parts[1], self.weights[1])
            self.done[slot] = total.astype(BF)
            self.store(index).start()

    def finish(self):
        for index in range(self.tiles - 2, self.tiles):
            self.store(jnp.int32(index)).wait()


def back_kernel(
    depth, tasks, images, groups, valid, block_order, order_ref, context_ref, query_ref, key_ref,
    value_ref, total_ref, mixed_grad_ref, cross_mixed_ref, tokens_ref, row_ref, gain_ref, qkv_ref,
    mixed_ref, self_total_ref, sum_ref, residual_ref, small_in_ref, all_w_ref, block_ref, left_ref, right_ref,
    *refs
):
    (
        context_grad_ref, query_grad_ref, update_ref, small_out_ref, gram_ref, block_far,
        key_grad, value_grad,
    ), refs = refs[:8], refs[8:]
    (
        context, context_t, key_acc, value_acc, cross_query_grad, self_mixed_grad, qkv_grad, weights,
        block_sem, weight_sem, context_sem,
    ), refs = refs[:11], refs[11:]
    context_back = ContextGrad(
        key_grad, value_grad, weights.at[pl.ds(3, 2)], context_grad_ref,
        refs[: ContextGrad.SCRATCH],
    )
    refs = refs[ContextGrad.SCRATCH :]
    chain = Chain(depth, tasks, refs[: Chain.SCRATCH])
    refs = refs[Chain.SCRATCH :]
    gram_acc = refs[7]
    step = pl.program_id(0)
    cross_steps = images * groups
    half = chain.half
    is_end = chain.is_end
    pairs = pairs_of(tasks)

    def add_products(shares):
        for index, (a, b) in enumerate(pairs):
            product = shares[a] * shares[b]
            total = product[0:8]
            for row in range(8, product.shape[0], 8):
                total = total + product[row : row + 8]
            gram_acc[index * 8 : index * 8 + 8] += total

    def unit(index):
        chain.unit(index)
        since = index - LAG * (depth - 1) - 3
        block = since // 2

        @pl.when(is_end & (since >= 0) & (since == 2 * block))
        def _():
            chain.wait_parts(block)
            for part in range(2):
                add_products(
                    [chain.parts[t, 2 * block + part].astype(F32) for t in range(tasks)]
                )

    block_copy = send(
        block_ref, block_far, block_sem.at[0], block_sem.at[1], tensor=1 - lax.axis_index("tensor")
    )
    weight_copies = [
        pltpu.make_async_copy(all_w_ref.at[source], weights.at[target], weight_sem.at[index])
        for index, (source, target) in enumerate(
            [(pl.ds(0, 5), pl.ds(0, 5)), (pl.ds(5, 2), pl.ds(3, 2))]
        )
    ]

    def context_copy(image):
        keys = context.shape[0]
        own = lax.axis_index("tensor") * images + image
        rows = pl.ds(pl.multiple_of(own * keys, keys), keys)
        return pltpu.make_async_copy(context_ref.at[0, rows], context, context_sem)

    @pl.when(step == 0)
    def _():
        context_copy(0).start()
        weight_copies[0].start()
        greet(depth, tasks)
        block_copy.start()
        gram_acc[...] = jnp.zeros_like(gram_acc)
        refs[0][...] = small_in_ref[...]

    @pl.when(step < cross_steps)
    def _():
        image = step // groups
        group = step - image * groups

        chain.emit(step, lambda lanes: mm(left_ref[0], right_ref[0, :, lanes]))

        @pl.when(group == 0)
        def _():
            context_copy(image).wait()
            context_t[...] = context[...].T

            @pl.when(image + 1 < images)
            def _():
                context_copy(image + 1).start()

        def cross_unit(part):
            if part == 0:
                chain.absorb(step)
            unit(step * UNITS + part)

        @pl.when(step > 0)
        def _():
            context_back.settle()

        grad_query = cross_back_step(
            image, group, query_ref, key_ref, value_ref, total_ref, mixed_grad_ref, cross_mixed_ref,
            refs[0], context_t, key_acc, value_acc, context_back.staged.at[0],
            context_back.staged.at[1], cross_unit,
        )
        context_back.put(image, group)
        rows = grad_query.shape[0]
        cross_query_grad[
            pl.ds(pl.multiple_of(image * rows, rows), rows),
            pl.ds(pl.multiple_of(group * SLAB, SLAB), SLAB),
        ] = grad_query

        @pl.when(step == cross_steps - 1)
        def _():
            chain.emit(cross_steps, lambda lanes: key_acc[:, lanes])
            chain.emit(cross_steps + 1, lambda lanes: value_acc[:, lanes])

    @pl.when(step == cross_steps)
    def _():
        done = [cross_steps * UNITS]
        blocks = len(block_order)

        def self_unit():
            if done[0] % 2 == 0:
                chain.absorb(done[0] // 2)
            unit(jnp.int32(done[0]))
            done[0] += 1

        in_loop = images * groups // 2

        def loop_unit(index):
            now = cross_steps * UNITS + 2 + index // 2

            @pl.when(index % 2 == 1)
            def _():
                @pl.when(now % 2 == 0)
                def _():
                    chain.absorb(now // 2)

                unit(now)

        def used():
            done[0] += in_loop
            weight_copies[1].start()

        context_back.settle()
        for copy in context_back.fetches(jnp.int32(0)):
            copy.start()
        weight_copies[0].wait()
        query_grad_ref[...] = self_back(
            images, valid, tokens_ref, weights, row_ref, gain_ref, qkv_ref, mixed_ref,
            self_total_ref, sum_ref, residual_ref, cross_query_grad, self_mixed_grad, refs[0],
            qkv_grad, lambda block, value: chain.emit(block_order.index(block), value), self_unit,
            loop_unit, used,
        ).astype(BF)
        for block in range(-(-done[0] // 2), blocks):
            chain.absorb(block)
        weight_copies[1].wait()
        rest(
            chain, unit, context_back, done[0], order_ref, update_ref, small_out_ref, gram_ref, refs
        )
        for block in range(blocks - STAGES, blocks):
            chain.far_copy(jnp.int32(block)).wait_send()
        block_copy.wait()
        context_back.finish()


def rest(
    chain, unit, context_back, done, order_ref, update_ref, small_out_ref, gram_ref, refs
):
    (
        small, small_own, small_other, small_far, small_pass, small_all, small_both, gram_acc,
        gram_plane, gram_end, out,
        small_far_sem, small_pass_sem, small_task_sem, small_dp_sem, small_core_sem,
        gram_plane_sem, gram_dp_sem, hop_sem, out_sem, update_sem,
    ) = refs
    depth, tasks, half = chain.depth, chain.tasks, chain.half
    me, task, core = (lax.axis_index(axis) for axis in ("dp", "task", "tensor"))
    is_end = chain.is_end
    top = me == 0
    pairs = pairs_of(tasks)
    own_lanes = pl.ds(pl.multiple_of(core * half, half), half)
    other_lanes = pl.ds(pl.multiple_of((1 - core) * half, half), half)
    small_own[0:8] = small[0:8, 0:half]
    small_own[8:] = small[8:, own_lanes]
    small_other[0:8] = small[0:8, half:]
    small_other[8:] = small[8:, other_lanes]
    small_copy = send(
        small_other, small_far, small_far_sem.at[0], small_far_sem.at[1], tensor=1 - core
    )
    small_copy.start()

    def small_hop():
        return send(
            small_pass, small_pass, small_pass_sem.at[0], small_pass_sem.at[1], dp=me - 1
        )

    def small_task_copy(shift, peer):
        return send(
            small_pass, small_all.at[task], small_task_sem.at[0, shift],
            small_task_sem.at[1, shift], task=peer,
        )

    def step(index, carry):
        unit(index)
        context_back.compute(index - done)

        @pl.when(index == done + 1 + LAG * chain.hops(0))
        def _():
            small_copy.wait_recv()
            total = small_own[...] + small_far[...]

            @pl.when(me == depth - 1)
            def _():
                small_pass[...] = total

            @pl.when(me < depth - 1)
            def _():
                small_hop().wait_recv()
                small_pass[...] += total

            @pl.when(me > 0)
            def _():
                small_hop().start()

            @pl.when(top)
            def _():
                for shift, peer in enumerate(task_peers(tasks)):
                    small_task_copy(shift, peer).start()
                small_all[task] = small_pass[...]

        return carry

    lax.fori_loop(done, max(chain.units() + 2, done + context_back.tiles), step, 0)

    @pl.when(top)
    def _():
        for shift, peer in enumerate(task_senders(tasks)):
            landed = small_all.at[peer]
            send(
                landed, landed, small_task_sem.at[0, shift], small_task_sem.at[1, shift], task=peer
            ).wait_recv()

    lanes = gram_plane.shape[2]
    plane = 2 * tasks
    mine = 2 * task + core

    def gram_copy(shift):
        to = lax.rem(mine + shift, plane)
        return send(
            gram_plane.at[mine], gram_plane.at[mine], gram_plane_sem.at[0, shift - 1],
            gram_plane_sem.at[1, shift - 1], task=to // 2, tensor=lax.rem(to, 2),
        )

    def gram_arrival(shift):
        place = lax.rem(mine + plane - shift, plane)
        return send(
            gram_plane.at[place], gram_plane.at[place], gram_plane_sem.at[0, shift - 1],
            gram_plane_sem.at[1, shift - 1], task=place // 2, tensor=lax.rem(place, 2),
        )

    def gram_dp_copy(end, shift):
        return send(
            gram_end.at[end], gram_end.at[end], gram_dp_sem.at[0, end, shift],
            gram_dp_sem.at[1, end, shift], dp=lax.rem((depth - 1) * end + shift + 1, depth),
        )

    def one_number(values):
        return jnp.sum(jnp.sum(values, axis=0, keepdims=True), axis=1, keepdims=True)

    @pl.when(top & (task == 0))
    def _():
        small_values = [small_all[t] for t in range(tasks)]
        for index, (a, b) in enumerate(pairs):
            product = small_values[a] * small_values[b]
            gram_acc[index * 8 : index * 8 + 8] += product[0:8] + product[8:16] + product[16:24]

    @pl.when(is_end)
    def _():
        gram_plane[mine] = jnp.zeros(gram_plane.shape[1:], F32)
        for index in range(len(pairs)):
            gram_plane[mine, index : index + 1] = jnp.broadcast_to(
                one_number(gram_acc[index * 8 : index * 8 + 8]), (1, lanes)
            )
        for shift in range(1, plane):
            gram_copy(shift).start()
        for shift in range(1, plane):
            gram_arrival(shift).wait_recv()

    for end in range(2):

        @pl.when(me == (depth - 1) * end)
        def _(end=end):
            total = gram_plane[0]
            for place in range(1, plane):
                total = total + gram_plane[place]
            gram_end[end] = total
            for shift in range(depth - 1):
                gram_dp_copy(end, shift).start()

    for end in range(2):
        for shift in range(depth - 1):

            @pl.when(me == ((depth - 1) * end + shift + 1) % depth)
            def _(end=end, shift=shift):
                gram_dp_copy(end, shift).wait_recv()

    gram = {}
    for index, (a, b) in enumerate(pairs):
        row = slice(index, index + 1)
        gram[a, b] = gram[b, a] = gram_end[0, row] + gram_end[1, row]
    for a in range(tasks):
        for b in range(tasks):
            gram_ref[a * tasks + b : a * tasks + b + 1] = gram[a, b]
    weights = [
        jnp.concatenate([weight] * (half // lanes), axis=1)
        for weight in weights_of(gram, order_ref, tasks)
    ]

    blocks = out.shape[0]
    group = blocks // GROUPS
    share = chain.rows // tasks
    own_share = pl.ds(pl.multiple_of(task * share, share), share)
    own_part = jnp.minimum(me, 1)

    def hop_copy(index):
        return send(
            chain.near.at[1, pl.ds(index * group, group), pl.ds(0, share)],
            out.at[pl.ds(index * group, group), own_share],
            hop_sem.at[0, index], hop_sem.at[1, index],
            dp=jnp.where(top, 1, depth - 2),
        )

    beside = [task + 1 - 2 * lax.rem(task, 2), task + 2 - 4 * (task // 2)]
    across = tasks - 1 - task

    def out_piece(index, owner):
        rows = pl.ds(pl.multiple_of(owner * share, share), share)
        return out.at[pl.ds(index * group, group), rows]

    def out_copy(index, which, owner):
        piece = out_piece(index, owner)
        peer = beside[which] if which < 2 else beside[1 if index < GROUPS // 2 else 0]
        return send(
            piece, piece, out_sem.at[0, index, which], out_sem.at[1, index, which], task=peer
        )

    def update_copy(index):
        at = pl.ds(index * group, group)
        return pltpu.make_async_copy(out.at[at], update_ref.at[at], update_sem.at[index])

    def weighted(chunk):
        total = weights[0] * chain.parts[0, chunk].astype(F32)
        for t in range(1, tasks):
            total = total + weights[t] * chain.parts[t, chunk].astype(F32)
        return total.astype(BF)

    def small_dp_copy(shift):
        return send(
            small_both.at[0], small_both.at[0], small_dp_sem.at[0, shift],
            small_dp_sem.at[1, shift], dp=shift + 1,
        )

    def small_core_copy():
        return send(
            small_both.at[0], small_both.at[1], small_core_sem.at[0], small_core_sem.at[1],
            tensor=1 - core,
        )

    @pl.when(top)
    def _():
        total = weights[0] * small_all[0]
        for t in range(1, tasks):
            total = total + weights[t] * small_all[t]
        small_both[0] = total
        for shift in range(depth - 1):
            small_dp_copy(shift).start()

    @pl.when(is_end)
    def _():
        for index in range(GROUPS):

            def other(block, carry):
                chain.near[1, block, 0:share] = weighted(2 * block + 1 - own_part)
                return carry

            lax.fori_loop(index * group, (index + 1) * group, other, 0)
            hop_copy(index).start()

            def own(block, carry):
                out[block, own_share] = weighted(2 * block + own_part)
                return carry

            lax.fori_loop(index * group, (index + 1) * group, own, 0)
            for which in range(2):
                out_copy(index, which, task).start()

    @pl.when(jnp.logical_not(is_end))
    def _():
        for index in range(GROUPS):
            hop_copy(index).wait_recv()
            for which in range(2):
                out_copy(index, which, task).start()

    for shift in range(depth - 1):

        @pl.when(me == shift + 1)
        def _(shift=shift):
            small_dp_copy(shift).wait_recv()

    small_core_copy().start()

    for index in range(GROUPS):
        for which in range(2):
            out_copy(index, which, beside[which]).wait_recv()
        out_copy(index, 2, beside[0 if index < GROUPS // 2 else 1]).start()
    for index in range(GROUPS):
        out_copy(index, 2, across).wait_recv()
        update_copy(index).start()

    small_core_copy().wait_recv()
    small_out_ref[0:8, 0:half] = small_both[0, 0:8]
    small_out_ref[0:8, half:] = small_both[1, 0:8]
    small_out_ref[8:, own_lanes] = small_both[0, 8:]
    small_out_ref[8:, other_lanes] = small_both[1, 8:]

    small_copy.wait_send()
    small_core_copy().wait_send()
    chain.finish()

    @pl.when(me > 0)
    def _():
        small_hop().wait_send()

    @pl.when(top)
    def _():
        for shift, peer in enumerate(task_peers(tasks)):
            small_task_copy(shift, peer).wait_send()
        for shift in range(depth - 1):
            small_dp_copy(shift).wait_send()

    for end in range(2):

        @pl.when(me == (depth - 1) * end)
        def _(end=end):
            for shift in range(depth - 1):
                gram_dp_copy(end, shift).wait_send()

    @pl.when(is_end)
    def _():
        for shift in range(1, plane):
            gram_copy(shift).wait_send()
        for index in range(GROUPS):
            hop_copy(index).wait_send()

    for index in range(GROUPS):
        update_copy(index).wait()
        for which in range(3):
            out_copy(index, which, task).wait_send()


def spread_kernel(
    images, valid, tasks, block_order, parts_ref, context_grad_ref, query_grad_ref, block_ref,
    block_far_ref, small_ref, gram_in_ref,
    update_ref, context_out_ref, query_out_ref, block_out_ref, head_ref, row_ref, gain_ref, gram_ref,
):
    ordered = [parts_ref[block_order.index(block)] for block in range(len(block_order))]
    update_ref[...] = jnp.swapaxes(jnp.stack(ordered), 0, 1).astype(F32)
    context_out_ref[...] = context_grad_ref[...]

    @pl.when(pl.program_id(0) == 0)
    def _():
        padded = query_grad_ref.shape[0] // images
        first = lax.axis_index("tensor") == 0

        def rows(ref, image):
            return ref[image * padded : (image + 1) * padded].astype(F32)[:valid]

        for image in range(images):
            at = slice(image * valid, (image + 1) * valid)
            after = slice((images + image) * valid, (images + image + 1) * valid)
            query_out_ref[at] = rows(query_grad_ref, image).astype(BF)
            near, far = rows(block_ref, image), rows(block_far_ref, image)
            block_out_ref[at] = jnp.where(first, near, far).astype(BF)
            block_out_ref[after] = jnp.where(first, far, near).astype(BF)
        head_ref[...] = small_ref[0:8, 0 : head_ref.shape[1]]
        for which in range(6):
            row_ref[which // 2, which % 2 : which % 2 + 1] = small_ref[8 + which : 9 + which]
        gain_ref[...] = small_ref[14:17]
        for a in range(tasks):
            for b in range(tasks):
                at = a * tasks + b
                gram_ref[a : a + 1, b : b + 1] = gram_in_ref[at : at + 1, 0:1]


def gram_kernel(parts_ref, gram_ref):
    tasks = parts_ref.shape[0]

    @pl.when(pl.program_id(0) == 0)
    def _():
        gram_ref[...] = jnp.zeros_like(gram_ref)

    shares = [parts_ref[task, 0].astype(F32) for task in range(tasks)]
    for a in range(tasks):
        for b in range(a, tasks):
            gram_ref[a * tasks + b : a * tasks + b + 1] += rows_sum(shares[a] * shares[b])


def update_kernel(weights_ref, parts_ref, update_ref):
    tasks, blocks = parts_ref.shape[:2]
    for block in range(blocks):
        total = weights_ref[0] * parts_ref[0, block].astype(F32)
        for task in range(1, tasks):
            total += weights_ref[task] * parts_ref[task, block].astype(F32)
        update_ref[:, block, :] = total


def body(
    queries, memory, cotangent, matches, counts, task_order, params, head_bias, row_bias, norm_gain
):
    all_images = matches.shape[1]
    valid = matches.shape[2]
    width = queries.shape[2]
    half = params.shape[2]
    block_count = params.shape[1]
    blocks = (block_count - 8) // 2
    cores = lax.axis_size("tensor")
    images = all_images // cores
    keys = memory.shape[1] // all_images
    padded = -(-valid // 16) * 16
    rows = images * padded
    groups = width // SLAB
    stack = GROUP * padded
    core = lax.axis_index("tensor")

    def const(shape, *index):
        return pl.BlockSpec(shape, lambda *_: index)

    total_shape = jax.ShapeDtypeStruct((images * groups, 8, stack), F32)
    low_rows = jax.ShapeDtypeStruct((rows, width), BF)
    full_rows = jax.ShapeDtypeStruct((rows, width), F32)
    small_shape = jax.ShapeDtypeStruct((24, width), F32)
    one_block = jax.ShapeDtypeStruct((width, width), BF)
    small_spec = const((24, width), 0, 0)
    row_spec = const(row_bias.shape, 0, 0, 0)
    gain_spec = const(norm_gain.shape, 0, 0)
    head_spec = const((16, width), 0, 0)
    rows_spec = const((rows, width), 0, 0)

    parts = 4
    part_blocks = block_count // 2
    raw_spec = const((None, *queries.shape[1:]), 0, 0, 0)
    (
        weights, head_rows, tokens, own_cotangent, qkv, self_mixed, self_total, first_sum,
        cross_query,
    ) = pl.pallas_call(
        functools.partial(start_kernel, images, valid),
        grid=(2 * parts,),
        out_shape=(
            jax.ShapeDtypeStruct((block_count, width, cores * half), BF),
            jax.ShapeDtypeStruct((16, cores * half), BF),
            low_rows, low_rows,
            jax.ShapeDtypeStruct((3, rows, width), BF), low_rows, total_shape, full_rows, low_rows,
        ),
        in_specs=[
            pl.BlockSpec((width // parts, part_blocks, half), lambda s: (s % parts, s // parts, 0)),
            const((8, half), 0, 0), raw_spec, raw_spec, row_spec, gain_spec,
        ],
        out_specs=(
            any_spec(), head_spec, rows_spec, rows_spec,
            const((3, rows, width), 0, 0, 0), rows_spec, const(total_shape.shape, 0, 0, 0),
            rows_spec, rows_spec,
        ),
        scratch_shapes=[
            pltpu.VMEM((part_blocks, width, cores * half), BF),
            pltpu.VMEM((part_blocks, width, half), BF),
            pltpu.VMEM((16, half), BF),
            pltpu.VMEM((16, cores * half), BF),
            pltpu.SemaphoreType.DMA((2 * parts + 1,)),
            pltpu.SemaphoreType.DMA((2 * parts + 1,)),
            pltpu.SemaphoreType.DMA((2 * parts,)),
            pltpu.SemaphoreType.DMA(()),
        ],
        compiler_params=params_for(collective_id=0, has_side_effects=True),
        name="start",
    )(params, head_bias, queries, cotangent, row_bias, norm_gain)

    def own_image(i, g):
        return 0, lax.axis_index("tensor") * images + i, 0

    context_all = pl.BlockSpec((None, keys, width), own_image)
    slab_q = pl.BlockSpec((padded, SLAB), lambda i, g: (i, g))
    slab_k = pl.BlockSpec((keys, SLAB), lambda i, g: (i, g))
    slab_t = pl.BlockSpec((1, 8, stack), lambda i, g: (i * groups + g, 0, 0))
    image_q = pl.BlockSpec((padded, width), lambda i: (i, 0))
    image_k = pl.BlockSpec((keys, width), lambda i: (i, 0))

    def slab_w(block):
        return pl.BlockSpec((1, width, SLAB), lambda i, g: (block, 0, g))

    key_rows = jax.ShapeDtypeStruct((images * keys, width), BF)
    key_slabs = jax.ShapeDtypeStruct((groups, images * keys, SLAB), BF)
    keys_act, values_act, cross_mixed, cross_total = pl.pallas_call(
        cross_kernel,
        grid=(images,),
        in_specs=[
            pl.BlockSpec((None, keys, width), lambda i: own_image(i, 0)),
            image_q, const((1, width, width), 5, 0, 0), const((1, width, width), 6, 0, 0), head_spec,
        ],
        out_specs=(
            image_k, image_k, image_q, pl.BlockSpec((groups, 8, stack), lambda i: (i, 0, 0)),
        ),
        out_shape=(key_rows, key_rows, low_rows, total_shape),
        compiler_params=params_for(),
        name="cross_forward",
    )(memory, cross_query, weights, weights, head_rows)

    per = 2 if blocks % 2 == 0 else 1
    block_rows, left, right, mixed_grad, second_grad, ffn_small = pl.pallas_call(
        functools.partial(ffn_kernel, images, blocks, per),
        grid=(2 * blocks // per,),
        out_shape=(
            low_rows,
            jax.ShapeDtypeStruct((3, width, rows), BF),
            jax.ShapeDtypeStruct((2 * blocks + 1, rows, width), BF),
            low_rows, full_rows, small_shape,
        ),
        in_specs=[
            rows_spec, rows_spec, rows_spec,
            const(matches.shape, 0, 0, 0),
            pl.BlockSpec(memory_space=pltpu.SMEM),
            const((1, width, width), 7, 0, 0),
            any_spec(), head_spec, row_spec, gain_spec,
        ],
        out_specs=(rows_spec, any_spec(), any_spec(), rows_spec, rows_spec, small_spec),
        scratch_shapes=[
            pltpu.VMEM((rows, width), F32),
            pltpu.VMEM((rows, width), BF),
            pltpu.VMEM((3, width, rows), BF),
            pltpu.VMEM((2 * blocks, rows, width), BF),
            pltpu.VMEM((blocks, rows, width), F32),
            pltpu.VMEM((rows, width), F32),
            pltpu.VMEM((rows, width), F32),
            pltpu.VMEM((8, width), F32),
            pltpu.VMEM((2, blocks, width, width), BF),
            pltpu.SemaphoreType.DMA((3,)),
            pltpu.SemaphoreType.DMA((2 * blocks + 1,)),
            pltpu.SemaphoreType.DMA((2, blocks // per)),
        ],
        compiler_params=params_for(),
        name="ffn",
    )(
        first_sum, cross_mixed, own_cotangent, matches, counts, weights, weights, head_rows, row_bias,
        norm_gain,
    )

    depth, tasks = lax.axis_size("dp"), lax.axis_size("task")
    by_chain = depth == 4 and tasks == 4 and cores == 2

    if by_chain:
        block_order = [*range(8, block_count), 7, 5, 6, 4, 3, 0, 1, 2]
        chain_rows = width // depth
        pair_rows = 8 * len(pairs_of(tasks))
        dma = pltpu.SemaphoreType.DMA
        last = images * groups - 1

        def at_step(make):
            def index_map(step):
                now = jnp.minimum(step, last)
                return make(now // groups, now - groups * (now // groups))

            return index_map

        def product(step):
            return jnp.minimum(step, 2 * blocks)

        def once(shape):
            return pl.BlockSpec(
                shape, lambda step: (0,) * len(shape), pipeline_mode=pl.Buffered(1)
            )

        step_q = pl.BlockSpec((padded, SLAB), at_step(lambda i, g: (i, g)))
        step_k = pl.BlockSpec((keys, SLAB), at_step(lambda i, g: (i, g)))

        small_half = pltpu.VMEM((24, half), F32)
        (
            context_grad, token_grad, update_parts, small_out, gram_rows, block_far, *_,
        ) = pl.pallas_call(
            functools.partial(
                back_kernel, depth, tasks, images, groups, valid, block_order
            ),
            grid=(images * groups + 1,),
            out_shape=(
                key_rows, low_rows,
                jax.ShapeDtypeStruct((block_count, chain_rows, half), BF),
                small_shape,
                jax.ShapeDtypeStruct((16, 128), F32),
                low_rows,
                key_slabs, key_slabs,
            ),
            in_specs=[
                pl.BlockSpec(memory_space=pltpu.SMEM),
                any_spec(), step_q, step_k, step_k,
                pl.BlockSpec((1, 8, stack), at_step(lambda i, g: (i * groups + g, 0, 0))),
                step_q, step_q,
                once((rows, width)), once(row_bias.shape), once(norm_gain.shape),
                once((3, rows, width)), once((rows, width)), once(total_shape.shape),
                once((rows, width)), once((rows, width)), once((24, width)),
                any_spec(), any_spec(),
                pl.BlockSpec((1, width, rows), lambda step: (product(step) // blocks, 0, 0)),
                pl.BlockSpec((1, rows, width), lambda step: (product(step), 0, 0)),
            ],
            out_specs=(
                any_spec(), once((rows, width)), any_spec(), once((24, width)), once((16, 128)),
                *[any_spec()] * 3,
            ),
            scratch_shapes=[
                pltpu.VMEM((keys, width), BF),
                pltpu.VMEM((width, keys), BF),
                pltpu.VMEM((width, width), F32),
                pltpu.VMEM((width, width), F32),
                pltpu.VMEM((rows, width), BF),
                pltpu.VMEM((rows, width), BF),
                pltpu.VMEM((3, rows, width), BF),
                pltpu.VMEM((5, width, width), BF),
                dma((2,)),
                dma((2,)),
                dma(()),
                *ContextGrad.scratch(keys, width),
                *Chain.scratch(block_count, chain_rows, half, tasks),
                pltpu.VMEM((24, width), F32),
                small_half, small_half, small_half, small_half,
                pltpu.VMEM((tasks, 24, half), F32),
                pltpu.VMEM((2, 24, half), F32),
                pltpu.VMEM((pair_rows, half), F32),
                pltpu.VMEM((2 * tasks, 16, 128), F32),
                pltpu.VMEM((2, 16, 128), F32),
                pltpu.VMEM((block_count, chain_rows, half), BF),
                dma((2,)),
                dma((2,)),
                dma((2, tasks - 1)),
                dma((2, depth - 1)),
                dma((2,)),
                dma((2, 2 * tasks - 1)),
                dma((2, 2, depth - 1)),
                dma((2, GROUPS)),
                dma((2, GROUPS, tasks - 1)),
                dma((GROUPS,)),
            ],
            compiler_params=params_for(collective_id=1, has_side_effects=True),
            name="backward",
        )(
            task_order, memory, cross_query, keys_act, values_act, cross_total, mixed_grad,
            cross_mixed, tokens, row_bias, norm_gain, qkv, self_mixed, self_total, first_sum,
            second_grad, ffn_small, weights, block_rows, left, right,
        )
        tile = chain_rows // images
        (
            param_update, memory_grad, query_grad, block_out, head_update, row_update, gain_update,
            gram,
        ) = pl.pallas_call(
            functools.partial(spread_kernel, images, valid, tasks, block_order),
            grid=(images,),
            out_shape=(
                jax.ShapeDtypeStruct((chain_rows, block_count, half), F32),
                key_rows,
                jax.ShapeDtypeStruct((images * valid, width), BF),
                jax.ShapeDtypeStruct((all_images * valid, width), BF),
                jax.ShapeDtypeStruct((8, half), F32),
                jax.ShapeDtypeStruct((3, 2, width), F32),
                jax.ShapeDtypeStruct((3, width), F32),
                jax.ShapeDtypeStruct((tasks, tasks), F32),
            ),
            in_specs=[
                pl.BlockSpec((block_count, tile, half), lambda r: (0, r, 0)),
                pl.BlockSpec((keys, width), lambda r: (r, 0)),
                rows_spec, rows_spec, rows_spec, small_spec, const((16, 128), 0, 0),
            ],
            out_specs=(
                pl.BlockSpec((tile, block_count, half), lambda r: (r, 0, 0)),
                pl.BlockSpec((keys, width), lambda r: (r, 0)),
                const((images * valid, width), 0, 0),
                const((all_images * valid, width), 0, 0),
                const((8, half), 0, 0), const((3, 2, width), 0, 0, 0),
                const((3, width), 0, 0), const((tasks, tasks), 0, 0),
            ),
            compiler_params=params_for(),
            name="spread",
        )(update_parts, context_grad, token_grad, block_rows, block_far, small_out, gram_rows)
        return (
            block_out[None], query_grad[None], memory_grad[None], param_update, head_update,
            row_update, gain_update, gram,
        )

    def unpad(array):
        return array.reshape(images, padded, width)[:, :valid].reshape(1, images * valid, width)

    block_out = lax.all_gather(unpad(block_rows), "tensor", axis=1, tiled=True)
    cross_query_grad, context_grad, key_wg, value_wg, cross_small = pl.pallas_call(
        cross_back_kernel,
        grid=(images, groups),
        in_specs=[
            context_all, slab_q, slab_k, slab_k, slab_t, slab_q, slab_q, slab_w(5), slab_w(6),
        ],
        out_specs=(
            slab_q,
            pl.BlockSpec((keys, width), lambda i, g: (i, 0)),
            const((width, width), 0, 0), const((width, width), 0, 0), small_spec,
        ),
        scratch_shapes=[
            pltpu.VMEM((width, keys), BF),
            pltpu.VMEM((keys, width), F32),
            pltpu.VMEM((width, width), F32),
            pltpu.VMEM((width, width), F32),
            pltpu.VMEM((keys, SLAB), BF),
            pltpu.VMEM((keys, SLAB), BF),
        ],
        out_shape=(low_rows, key_rows, one_block, one_block, small_shape),
        compiler_params=params_for(),
        name="cross_backward",
    )(
        memory, cross_query, keys_act, values_act, cross_total, mixed_grad, cross_mixed, weights,
        weights,
    )

    token_grad, self_wg, self_small = pl.pallas_call(
        functools.partial(self_back_kernel, images, valid),
        grid=(1,),
        out_shape=(
            low_rows, jax.ShapeDtypeStruct((5, width, width), BF), small_shape,
        ),
        in_specs=[
            rows_spec, const((5, width, width), 0, 0, 0), row_spec, gain_spec,
            const((3, rows, width), 0, 0, 0), rows_spec, const(total_shape.shape, 0, 0, 0),
            rows_spec, rows_spec, rows_spec,
        ],
        out_specs=(
            rows_spec, const((5, width, width), 0, 0, 0), small_spec,
        ),
        scratch_shapes=[pltpu.VMEM((3, rows, width), BF), pltpu.VMEM((rows, width), BF)],
        compiler_params=params_for(),
        name="self_backward",
    )(
        tokens, weights, row_bias, norm_gain, qkv, self_mixed, self_total, first_sum, second_grad,
        cross_query_grad,
    )

    query_grad = unpad(token_grad)
    memory_grad = context_grad[None]

    small = self_small + cross_small + ffn_small
    product = functools.partial(jnp.einsum, "dr,jre->jde", preferred_element_type=F32)
    grad_in = product(left[0], right[:blocks]).astype(BF)
    grad_out = product(left[1], right[blocks : 2 * blocks]).astype(BF)
    cross_out_wg = product(left[2], right[2 * blocks :])[0].astype(BF)
    grads = jnp.concatenate(
        [self_wg, jnp.stack([key_wg, value_wg, cross_out_wg]), grad_in, grad_out], axis=0
    )
    swap = [(0, 1), (1, 0)]
    grads = (
        grads[:, :, :half].astype(F32) + lax.ppermute(grads[:, :, half:], "tensor", swap).astype(F32)
    ).astype(BF)
    head_small = small[:8, :half] + lax.ppermute(small[:8, half:], "tensor", swap)
    row_small = lax.psum(small[8:17], ("dp", "tensor"))
    head_small = lax.psum(head_small, "dp")
    shard = lax.psum_scatter(grads, "dp", scatter_dimension=1, tiled=True)
    all_shards = lax.all_gather(shard, "task", axis=0, tiled=False)
    all_head = lax.all_gather(head_small, "task", axis=0, tiled=False)
    all_row = lax.all_gather(row_small, "task", axis=0, tiled=False)
    tasks = all_shards.shape[0]
    share_rows = shard.shape[1]
    sums = pl.pallas_call(
        gram_kernel,
        grid=(block_count,),
        out_shape=jax.ShapeDtypeStruct((tasks * tasks, half), F32),
        in_specs=[pl.BlockSpec((tasks, 1, share_rows, half), lambda k: (0, k, 0, 0))],
        out_specs=const((tasks * tasks, half), 0, 0),
        compiler_params=params_for(),
        name="gram",
    )(all_shards)
    upper = jnp.sum(sums, axis=1).reshape(tasks, tasks)
    gram_weights = upper + upper.T - jnp.diag(jnp.diag(upper))
    gram_weights = lax.psum(gram_weights, ("dp", "tensor"))
    gram_heads = jnp.einsum("axy,bxy->ab", all_head, all_head, precision=highest)
    gram_heads = lax.psum(gram_heads, "tensor")
    gram = gram_weights + gram_heads + jnp.einsum(
        "axy,bxy->ab", all_row, all_row, precision=highest
    )
    task_weights = combine_weights(gram, task_order)
    tile = 64 if share_rows % 64 == 0 else share_rows
    param_update = pl.pallas_call(
        update_kernel,
        grid=(share_rows // tile,),
        out_shape=jax.ShapeDtypeStruct((share_rows, block_count, half), F32),
        in_specs=[
            pl.BlockSpec(memory_space=pltpu.SMEM),
            pl.BlockSpec((tasks, block_count, tile, half), lambda r: (0, 0, r, 0)),
        ],
        out_specs=pl.BlockSpec((tile, block_count, half), lambda r: (r, 0, 0)),
        compiler_params=params_for(),
        name="update",
    )(task_weights, all_shards)
    head_bias_update = jnp.einsum("a,axy->xy", task_weights, all_head, precision=highest)
    row_update = jnp.einsum("a,axy->xy", task_weights, all_row, precision=highest)
    return (
        block_out, query_grad, memory_grad, param_update, head_bias_update,
        row_update[:6].reshape(3, 2, width), row_update[6:9], gram,
    )


def solution(mesh):
    return jax.shard_map(
        body,
        mesh=mesh,
        in_specs=(
            P("task", "dp", None),
            P("task", "dp", None),
            P("task", "dp", None),
            P("task", "dp", None),
            P("task", "dp"),
            P(),
            P(None, None, "tensor"),
            P(None, "tensor"),
            P(),
            P(),
        ),
        out_specs=(
            P("task", "dp", None),
            P("task", ("dp", "tensor"), None),
            P("task", ("dp", "tensor"), None),
            P("dp", None, "tensor"),
            P(None, "tensor"),
            P(),
            P(),
            P(),
        ),
        check_vma=False,
    )
```

profile of v0, /device:TPU:8, one launch (start us, length us, event | category | flops | bytes accessed | tf_op | source)
XLA Modules:
  0.0 260.9 jit_solution(3137616287239766375)
XLA Ops:
  0.6 1.3 copy.18.matches_ref
  1.9 19.5 %start.1 = (bf16[16,768,768]{2,1,0:T(8,128)(2,1)}, bf16[16,768]{1,0:T(8,128)(2,1)}, bf16[336,768]{1,0:T(8,128)(2,1)}, bf16[336,768]{1,0:T(8,128)(2,1)}, bf16[3,3...) custom-call(bf16[768,16,384]{2,1,0:T(8,128)(2,1)} %own_ref.1, ...), custom_call_target="tpu_custom_call" | custom-call | tf_op jit(solution)/shard_map/start/pallas_call | solution.py:1500
  21.4 23.7 %cross_forward.1 = (bf16[3600,768]{1,0:T(8,128)(2,1)}, bf16[3600,768]{1,0:T(8,128)(2,1)}, bf16[336,768]{1,0:T(8,128)(2,1)}, f32[9,8,448]{2,1,0:T(8,128)}) custom-call(bf16[1,7200,768]{2,1,0:T(8,128)(2,1)} %context_ref.3, bf16[336,768]{1,0:T(8,128)(2,1)} %get-tuple-element.41.query_ref, ...), custom_call_target="tpu_custom_call" | custom-call | tf_op jit(solution)/shard_map/cross_forward/pallas_call | solution.py:1547
  45.2 18.5 %ffn.1 = (bf16[336,768]{1,0:T(8,128)(2,1)}, bf16[3,768,336]{2,1,0:T(8,128)(2,1)}, bf16[9,336,768]{2,1,0:T(8,128)(2,1)}, bf16[336,768]{1,0:T(8,128)(2,1)}, f32[336,768]{1,0:T(8,128)}, /*index=5*/f32[24,768]{1,0:T(8,128)}) custom-call(f32[336,768]{1,0:T(8,128)} %get-tuple-element.47.sum_ref, bf16[336,768]{1,0:T(8,128)(2,1)} %get-tuple-element.48.mixed_ref.cross_mixed_ref, ...), custom_call_target="tpu_custom_call" | custom-call | tf_op jit(solution)/shard_map/ffn/pallas_call | solution.py:1563
  63.8 187.6 %backward.1 = (bf16[3600,768]{1,0:T(8,128)(2,1)}, bf16[336,768]{1,0:T(8,128)(2,1)}, bf16[16,192,384]{2,1,0:T(8,128)(2,1)}, f32[24,768]{1,0:T(8,128)}, f32[16,128...) custom-call(s32[4]{0:T(128)} %order_ref.1, ...), custom_call_target="tpu_custom_call" | custom-call | tf_op jit(solution)/shard_map/backward/pallas_call | solution.py:1632
  251.4 9.3 %spread.1 = (f32[192,16,384]{2,1,0:T(8,128)}, bf16[3600,768]{1,0:T(8,128)(2,1)}, bf16[300,768]{1,0:T(8,128)(2,1)}, bf16[600,768]{1,0:T(8,128)(2,1)}, f32[8,384]{...) custom-call(bf16[16,192,384]{2,1,0:T(8,128)(2,1)} %get-tuple-element.60.parts_ref, ...), custom_call_target="tpu_custom_call" | custom-call | tf_op jit(solution)/shard_map/spread/pallas_call | solution.py:1705
where the time goes:
time: 264 us; the launch traced here: 261 us
  Pallas kernels  259 us (98%)
    pallas_call x1, Pallas kernels, body(): pl.pallas_call(functools.partial(back_kernel, depth, tasks, images, group...  188 us
    pallas_call x1, Pallas kernels, body(): pl.pallas_call(cross_kernel, grid=(images,), in_specs=[pl.BlockSpec((None...  23.7 us
    pallas_call x1, Pallas kernels, body(): pl.pallas_call(functools.partial(start_kernel, images, valid), grid=(2 *...  19.5 us
    pallas_call x1, Pallas kernels, body(): pl.pallas_call(functools.partial(ffn_kernel, images, blocks, per), grid=(...  18.5 us
    pallas_call x1, Pallas kernels, body(): pl.pallas_call(functools.partial(spread_kernel, images, valid, tasks, blo...  9.28 us

commit v1 on v0

--- a/solution.py
+++ b/solution.py
@@ -730,9 +730,7 @@
         self.far_copy(block).wait_recv()
         for way in range(2):
             chunks = pl.ds(2 * block, 2)
-            self.near[way, chunks] = (
-                self.near[way, chunks].astype(F32) + self.far[slot, way].astype(F32)
-            ).astype(BF)
+            self.near[way, chunks] = self.near[way, chunks] + self.far[slot, way]
 
         @pl.when(block < self.chunks // 2 - SLOTS)
         def _():
@@ -785,9 +783,7 @@
         @pl.when(jnp.logical_not(first))
         def _():
             self.pass_copy(way, chunk).wait_recv()
-            self.passed[way, chunk] = (
-                own.astype(F32) + self.passed[way, chunk].astype(F32)
-            ).astype(BF)
+            self.passed[way, chunk] = own + self.passed[way, chunk]
 
         @pl.when(jnp.logical_not(last))
         def _():
@@ -850,7 +846,7 @@
     return totals
 
 
-GROUPS = 4
+GROUPS = 8
 UNITS = 2
 TILE = 240
 
@@ -971,27 +967,6 @@
     is_end = chain.is_end
     pairs = pairs_of(tasks)
 
-    def add_products(shares):
-        for index, (a, b) in enumerate(pairs):
-            product = shares[a] * shares[b]
-            total = product[0:8]
-            for row in range(8, product.shape[0], 8):
-                total = total + product[row : row + 8]
-            gram_acc[index * 8 : index * 8 + 8] += total
-
-    def unit(index):
-        chain.unit(index)
-        since = index - LAG * (depth - 1) - 3
-        block = since // 2
-
-        @pl.when(is_end & (since >= 0) & (since == 2 * block))
-        def _():
-            chain.wait_parts(block)
-            for part in range(2):
-                add_products(
-                    [chain.parts[t, 2 * block + part].astype(F32) for t in range(tasks)]
-                )
-
     block_copy = send(
         block_ref, block_far, block_sem.at[0], block_sem.at[1], tensor=1 - lax.axis_index("tensor")
     )
@@ -1036,7 +1011,7 @@
         def cross_unit(part):
             if part == 0:
                 chain.absorb(step)
-            unit(step * UNITS + part)
+            chain.unit(step * UNITS + part)
 
         @pl.when(step > 0)
         def _():
@@ -1067,7 +1042,7 @@
         def self_unit():
             if done[0] % 2 == 0:
                 chain.absorb(done[0] // 2)
-            unit(jnp.int32(done[0]))
+            chain.unit(jnp.int32(done[0]))
             done[0] += 1
 
         in_loop = images * groups // 2
@@ -1081,7 +1056,7 @@
                 def _():
                     chain.absorb(now // 2)
 
-                unit(now)
+                chain.unit(now)
 
         def used():
             done[0] += in_loop
@@ -1101,7 +1076,7 @@
             chain.absorb(block)
         weight_copies[1].wait()
         rest(
-            chain, unit, context_back, done[0], order_ref, update_ref, small_out_ref, gram_ref, refs
+            chain, context_back, done[0], order_ref, update_ref, small_out_ref, gram_ref, refs
         )
         for block in range(blocks - STAGES, blocks):
             chain.far_copy(jnp.int32(block)).wait_send()
@@ -1110,7 +1085,7 @@
 
 
 def rest(
-    chain, unit, context_back, done, order_ref, update_ref, small_out_ref, gram_ref, refs
+    chain, context_back, done, order_ref, update_ref, small_out_ref, gram_ref, refs
 ):
     (
         small, small_own, small_other, small_far, small_pass, small_all, small_both, gram_acc,
@@ -1145,9 +1120,40 @@
             small_task_sem.at[1, shift], task=peer,
         )
 
+    def add_products(shares):
+        for index, (a, b) in enumerate(pairs):
+            product = shares[a] * shares[b]
+            total = product[0:8]
+            for row in range(8, product.shape[0], 8):
+                total = total + product[row : row + 8]
+            gram_acc[index * 8 : index * 8 + 8] += total
+
+    blocks = chain.chunks // 2
+    late = LAG * (depth - 1) + 3
+
+    def products_of(block):
+        @pl.when((block >= 0) & (block < blocks))
+        def _():
+            chain.wait_parts(block)
+
+            def part(which, carry):
+                add_products(
+                    [chain.parts[t, 2 * block + which].astype(F32) for t in range(tasks)]
+                )
+                return carry
+
+            lax.fori_loop(0, 2, part, 0)
+
     def step(index, carry):
-        unit(index)
+        chain.unit(index)
         context_back.compute(index - done)
+        since = index - late
+
+        @pl.when(is_end)
+        def _():
+            early = (done - late) // 2 + 1
+            products_of(jnp.where(index - done < early, index - done, -1))
+            products_of(jnp.where(since == 2 * (since // 2), since // 2, -1))
 
         @pl.when(index == done + 1 + LAG * chain.hops(0))
         def _():
@@ -1261,7 +1267,6 @@
         for weight in weights_of(gram, order_ref, tasks)
     ]
 
-    blocks = out.shape[0]
     group = blocks // GROUPS
     share = chain.rows // tasks
     own_share = pl.ds(pl.multiple_of(task * share, share), share)

time: 264 us -> 260 us (0.985)
  Pallas kernels: 259 us -> 255 us
    pallas_call x1, Pallas kernels: 188 us -> 184 us  [body(): pl.pallas_call(functools.partial(back_kernel, depth, tasks, images, group...]
where the time goes in v1:
time: 260 us; the launch traced here: 257 us
  Pallas kernels  255 us (98%)
    pallas_call x1, Pallas kernels, body(): pl.pallas_call(functools.partial(back_kernel, depth, tasks, images, group...  184 us
    pallas_call x1, Pallas kernels, body(): pl.pallas_call(cross_kernel, grid=(images,), in_specs=[pl.BlockSpec((None...  23.7 us
    pallas_call x1, Pallas kernels, body(): pl.pallas_call(functools.partial(start_kernel, images, valid), grid=(2 *...  19.5 us
    pallas_call x1, Pallas kernels, body(): pl.pallas_call(functools.partial(ffn_kernel, images, blocks, per), grid=(...  18.5 us
    pallas_call x1, Pallas kernels, body(): pl.pallas_call(functools.partial(spread_kernel, images, valid, tasks, blo...  9.28 us

profile of v1, /device:TPU:8, one launch (start us, length us, event | category | flops | bytes accessed | tf_op | source)
XLA Modules:
  0.0 257.1 jit_solution(10487625677507475964)
XLA Ops:
  0.6 1.3 copy.18.matches_ref
  1.9 19.5 %start.1 = (bf16[16,768,768]{2,1,0:T(8,128)(2,1)}, bf16[16,768]{1,0:T(8,128)(2,1)}, bf16[336,768]{1,0:T(8,128)(2,1)}, bf16[336,768]{1,0:T(8,128)(2,1)}, bf16[3,3...) custom-call(bf16[768,16,384]{2,1,0:T(8,128)(2,1)} %own_ref.1, ...), custom_call_target="tpu_custom_call" | custom-call | tf_op jit(solution)/shard_map/start/pallas_call | solution.py:1505
  21.4 23.7 %cross_forward.1 = (bf16[3600,768]{1,0:T(8,128)(2,1)}, bf16[3600,768]{1,0:T(8,128)(2,1)}, bf16[336,768]{1,0:T(8,128)(2,1)}, f32[9,8,448]{2,1,0:T(8,128)}) custom-call(bf16[1,7200,768]{2,1,0:T(8,128)(2,1)} %context_ref.3, bf16[336,768]{1,0:T(8,128)(2,1)} %get-tuple-element.41.query_ref, ...), custom_call_target="tpu_custom_call" | custom-call | tf_op jit(solution)/shard_map/cross_forward/pallas_call | solution.py:1552
  45.2 18.5 %ffn.1 = (bf16[336,768]{1,0:T(8,128)(2,1)}, bf16[3,768,336]{2,1,0:T(8,128)(2,1)}, bf16[9,336,768]{2,1,0:T(8,128)(2,1)}, bf16[336,768]{1,0:T(8,128)(2,1)}, f32[336,768]{1,0:T(8,128)}, /*index=5*/f32[24,768]{1,0:T(8,128)}) custom-call(f32[336,768]{1,0:T(8,128)} %get-tuple-element.47.sum_ref, bf16[336,768]{1,0:T(8,128)(2,1)} %get-tuple-element.48.mixed_ref.cross_mixed_ref, ...), custom_call_target="tpu_custom_call" | custom-call | tf_op jit(solution)/shard_map/ffn/pallas_call | solution.py:1568
  63.8 183.8 %backward.1 = (bf16[3600,768]{1,0:T(8,128)(2,1)}, bf16[336,768]{1,0:T(8,128)(2,1)}, bf16[16,192,384]{2,1,0:T(8,128)(2,1)}, f32[24,768]{1,0:T(8,128)}, f32[16,128...) custom-call(s32[4]{0:T(128)} %order_ref.1, ...), custom_call_target="tpu_custom_call" | custom-call | tf_op jit(solution)/shard_map/backward/pallas_call | solution.py:1637
  247.6 9.3 %spread.1 = (f32[192,16,384]{2,1,0:T(8,128)}, bf16[3600,768]{1,0:T(8,128)(2,1)}, bf16[300,768]{1,0:T(8,128)(2,1)}, bf16[600,768]{1,0:T(8,128)(2,1)}, f32[8,384]{...) custom-call(bf16[16,192,384]{2,1,0:T(8,128)(2,1)} %get-tuple-element.60.parts_ref, ...), custom_call_target="tpu_custom_call" | custom-call | tf_op jit(solution)/shard_map/spread/pallas_call | solution.py:1710

commit v2 on v1

--- a/solution.py
+++ b/solution.py
@@ -132,7 +132,7 @@
     return grad_query.astype(BF), grad_key.astype(BF), grad_value.astype(BF)
 
 
-KEY_TILE = 400
+KEY_TILE = 1200
 
 
 def attend_back_tiles(
@@ -420,7 +420,7 @@
         grads = []
         for image in range(images):
             own = lax.axis_index("tensor") * images + image
-            live = (matches_ref[0, pl.ds(own, 1)] == slot) & (box < counts_ref[0, own])
+            live = (matches_ref[own] == slot) & (box < counts_ref[0, own])
             mask = jnp.sum(jnp.where(live, 1.0, 0.0), axis=1, keepdims=True)
             cot = cotangent_ref[image * rows : (image + 1) * rows].astype(F32)
             grads.append(cot * mask)
@@ -1010,6 +1010,7 @@
 
         def cross_unit(part):
             if part == 0:
+                context_back.put(image, group)
                 chain.absorb(step)
             chain.unit(step * UNITS + part)
 
@@ -1022,7 +1023,6 @@
             refs[0], context_t, key_acc, value_acc, context_back.staged.at[0],
             context_back.staged.at[1], cross_unit,
         )
-        context_back.put(image, group)
         rows = grad_query.shape[0]
         cross_query_grad[
             pl.ds(pl.multiple_of(image * rows, rows), rows),
@@ -1576,7 +1576,7 @@
         ),
         in_specs=[
             rows_spec, rows_spec, rows_spec,
-            const(matches.shape, 0, 0, 0),
+            const((all_images, 1, valid), 0, 0, 0),
             pl.BlockSpec(memory_space=pltpu.SMEM),
             const((1, width, width), 7, 0, 0),
             any_spec(), head_spec, row_spec, gain_spec,
@@ -1599,7 +1599,7 @@
         compiler_params=params_for(),
         name="ffn",
     )(
-        first_sum, cross_mixed, own_cotangent, matches, counts, weights, weights, head_rows, row_bias,
+        first_sum, cross_mixed, own_cotangent, jnp.transpose(matches, (1, 0, 2)), counts, weights, weights, head_rows, row_bias,
         norm_gain,
     )
 

time: 260 us -> 257 us (0.988)
  no operation moved by 1% of the time
where the time goes in v2:
time: 257 us; the launch traced here: 255 us
  Pallas kernels  254 us (99%)
    pallas_call x1, Pallas kernels, body(): pl.pallas_call(functools.partial(back_kernel, depth, tasks, images, group...  183 us
    pallas_call x1, Pallas kernels, body(): pl.pallas_call(cross_kernel, grid=(images,), in_specs=[pl.BlockSpec((None...  23.7 us
    pallas_call x1, Pallas kernels, body(): pl.pallas_call(functools.partial(start_kernel, images, valid), grid=(2 *...  19.6 us
    pallas_call x1, Pallas kernels, body(): pl.pallas_call(functools.partial(ffn_kernel, images, blocks, per), grid=(...  18.5 us
    pallas_call x1, Pallas kernels, body(): pl.pallas_call(functools.partial(spread_kernel, images, valid, tasks, blo...  9.28 us

profile of v2, /device:TPU:8, one launch (start us, length us, event | category | flops | bytes accessed | tf_op | source)
XLA Modules:
  0.0 254.7 jit_solution(854889352263091043)
XLA Ops:
  0.6 19.6 %start.1 = (bf16[16,768,768]{2,1,0:T(8,128)(2,1)}, bf16[16,768]{1,0:T(8,128)(2,1)}, bf16[336,768]{1,0:T(8,128)(2,1)}, bf16[336,768]{1,0:T(8,128)(2,1)}, bf16[3,3...) custom-call(bf16[768,16,384]{2,1,0:T(8,128)(2,1)} %own_ref.1, ...), custom_call_target="tpu_custom_call" | custom-call | tf_op jit(solution)/shard_map/start/pallas_call | solution.py:1505
  20.2 23.7 %cross_forward.1 = (bf16[3600,768]{1,0:T(8,128)(2,1)}, bf16[3600,768]{1,0:T(8,128)(2,1)}, bf16[336,768]{1,0:T(8,128)(2,1)}, f32[9,8,448]{2,1,0:T(8,128)}) custom-call(bf16[1,7200,768]{2,1,0:T(8,128)(2,1)} %context_ref.3, bf16[336,768]{1,0:T(8,128)(2,1)} %get-tuple-element.41.query_ref, ...), custom_call_target="tpu_custom_call" | custom-call | tf_op jit(solution)/shard_map/cross_forward/pallas_call | solution.py:1552
  44.0 18.5 %ffn.1 = (bf16[336,768]{1,0:T(8,128)(2,1)}, bf16[3,768,336]{2,1,0:T(8,128)(2,1)}, bf16[9,336,768]{2,1,0:T(8,128)(2,1)}, bf16[336,768]{1,0:T(8,128)(2,1)}, f32[336,768]{1,0:T(8,128)}, /*index=5*/f32[24,768]{1,0:T(8,128)}) custom-call(f32[336,768]{1,0:T(8,128)} %get-tuple-element.47.sum_ref, bf16[336,768]{1,0:T(8,128)(2,1)} %get-tuple-element.48.mixed_ref.cross_mixed_ref, ...), custom_call_target="tpu_custom_call" | custom-call | tf_op jit(solution)/shard_map/ffn/pallas_call | solution.py:1568
  62.5 182.7 %backward.1 = (bf16[3600,768]{1,0:T(8,128)(2,1)}, bf16[336,768]{1,0:T(8,128)(2,1)}, bf16[16,192,384]{2,1,0:T(8,128)(2,1)}, f32[24,768]{1,0:T(8,128)}, f32[16,128...) custom-call(s32[4]{0:T(128)} %order_ref.1, ...), custom_call_target="tpu_custom_call" | custom-call | tf_op jit(solution)/shard_map/backward/pallas_call | solution.py:1637
  245.2 9.3 %spread.1 = (f32[192,16,384]{2,1,0:T(8,128)}, bf16[3600,768]{1,0:T(8,128)(2,1)}, bf16[300,768]{1,0:T(8,128)(2,1)}, bf16[600,768]{1,0:T(8,128)(2,1)}, f32[8,384]{...) custom-call(bf16[16,192,384]{2,1,0:T(8,128)(2,1)} %get-tuple-element.60.parts_ref, ...), custom_call_target="tpu_custom_call" | custom-call | tf_op jit(solution)/shard_map/spread/pallas_call | solution.py:1710

commit v3 on v2

--- a/solution.py
+++ b/solution.py
@@ -846,7 +846,7 @@
     return totals
 
 
-GROUPS = 8
+GROUPS = 16
 UNITS = 2
 TILE = 240
 

time: 257 us -> 257 us (level)
  no operation moved by 1% of the time
where the time goes in v3:
time: 257 us; the launch traced here: 255 us
  Pallas kernels  254 us (99%)
    pallas_call x1, Pallas kernels, body(): pl.pallas_call(functools.partial(back_kernel, depth, tasks, images, group...  183 us
    pallas_call x1, Pallas kernels, body(): pl.pallas_call(cross_kernel, grid=(images,), in_specs=[pl.BlockSpec((None...  23.7 us
    pallas_call x1, Pallas kernels, body(): pl.pallas_call(functools.partial(start_kernel, images, valid), grid=(2 *...  19.6 us
    pallas_call x1, Pallas kernels, body(): pl.pallas_call(functools.partial(ffn_kernel, images, blocks, per), grid=(...  18.5 us
    pallas_call x1, Pallas kernels, body(): pl.pallas_call(functools.partial(spread_kernel, images, valid, tasks, blo...  9.28 us

profile of v3, /device:TPU:8, one launch (start us, length us, event | category | flops | bytes accessed | tf_op | source)
XLA Modules:
  0.0 255.0 jit_solution(11893868559656525414)
XLA Ops:
  0.6 19.6 %start.1 = (bf16[16,768,768]{2,1,0:T(8,128)(2,1)}, bf16[16,768]{1,0:T(8,128)(2,1)}, bf16[336,768]{1,0:T(8,128)(2,1)}, bf16[336,768]{1,0:T(8,128)(2,1)}, bf16[3,3...) custom-call(bf16[768,16,384]{2,1,0:T(8,128)(2,1)} %own_ref.1, ...), custom_call_target="tpu_custom_call" | custom-call | tf_op jit(solution)/shard_map/start/pallas_call | solution.py:1505
  20.2 23.7 %cross_forward.1 = (bf16[3600,768]{1,0:T(8,128)(2,1)}, bf16[3600,768]{1,0:T(8,128)(2,1)}, bf16[336,768]{1,0:T(8,128)(2,1)}, f32[9,8,448]{2,1,0:T(8,128)}) custom-call(bf16[1,7200,768]{2,1,0:T(8,128)(2,1)} %context_ref.3, bf16[336,768]{1,0:T(8,128)(2,1)} %get-tuple-element.41.query_ref, ...), custom_call_target="tpu_custom_call" | custom-call | tf_op jit(solution)/shard_map/cross_forward/pallas_call | solution.py:1552
  44.0 18.5 %ffn.1 = (bf16[336,768]{1,0:T(8,128)(2,1)}, bf16[3,768,336]{2,1,0:T(8,128)(2,1)}, bf16[9,336,768]{2,1,0:T(8,128)(2,1)}, bf16[336,768]{1,0:T(8,128)(2,1)}, f32[336,768]{1,0:T(8,128)}, /*index=5*/f32[24,768]{1,0:T(8,128)}) custom-call(f32[336,768]{1,0:T(8,128)} %get-tuple-element.47.sum_ref, bf16[336,768]{1,0:T(8,128)(2,1)} %get-tuple-element.48.mixed_ref.cross_mixed_ref, ...), custom_call_target="tpu_custom_call" | custom-call | tf_op jit(solution)/shard_map/ffn/pallas_call | solution.py:1568
  62.5 183.0 %backward.1 = (bf16[3600,768]{1,0:T(8,128)(2,1)}, bf16[336,768]{1,0:T(8,128)(2,1)}, bf16[16,192,384]{2,1,0:T(8,128)(2,1)}, f32[24,768]{1,0:T(8,128)}, f32[16,128...) custom-call(s32[4]{0:T(128)} %order_ref.1, ...), custom_call_target="tpu_custom_call" | custom-call | tf_op jit(solution)/shard_map/backward/pallas_call | solution.py:1637
  245.6 9.3 %spread.1 = (f32[192,16,384]{2,1,0:T(8,128)}, bf16[3600,768]{1,0:T(8,128)(2,1)}, bf16[300,768]{1,0:T(8,128)(2,1)}, bf16[600,768]{1,0:T(8,128)(2,1)}, f32[8,384]{...) custom-call(bf16[16,192,384]{2,1,0:T(8,128)(2,1)} %get-tuple-element.60.parts_ref, ...), custom_call_target="tpu_custom_call" | custom-call | tf_op jit(solution)/shard_map/spread/pallas_call | solution.py:1710
